TPU v7x, 256 devices: a whole 4x4x8 slice. The times are simulated.
256 devices in a mesh: row: 16 (over z, core), col: 16 (over x, y).
Axes of the slice: x: 4, y: 4, z: 8, core: 2. Of those that a mesh axis runs over, the one named last changes fastest.
Arguments:
- tokens: bfloat16 [1024, 6144], P('col', 'row'), may hold values from -6 to 6
- w_in: bfloat16 [6144, 24576], P('row', 'col'), may hold values from -0.078125 to 0.078125
- w_out: bfloat16 [24576, 6144], P('col', 'row'), may hold values from -0.0390625 to 0.0390625
- d_output: bfloat16 [1024, 6144], P('col', 'row'), may hold values from -6 to 6
Outputs:
- output: float32 [1024, 6144], P('col', 'row')
- grad_tokens: float32 [1024, 6144], P('col', 'row')
- grad_w_in: float32 [6144, 24576], P('row', 'col')
- grad_w_out: float32 [24576, 6144], P('col', 'row')
All inputs are finite; a program needn't handle non-finite values.
Results may differ from a plain program's by a relative error of at most 0.0029.
Values may be sent and summed in bfloat16 or wider, within the bound.
A program may use at most 128 MiB of HBM per device.

v0:
```python
import jax
import jax.numpy as jnp
from jax import lax
from jax.sharding import PartitionSpec as P


def gelu_exact(values):
    return values * 0.5 * (1.0 + lax.erf(values * 0.7071067811865476))


def gelu_slope(values):
    normal_cdf = 0.5 * (1.0 + lax.erf(values * 0.7071067811865476))
    return normal_cdf + values * jnp.exp(-0.5 * values * values) * 0.3989422804014327


def shards(tokens, w_in, w_out, d_output):
    gathered = lax.all_gather(tokens, "col", axis=0, tiled=True)
    partial_hidden = jnp.dot(gathered, w_in, preferred_element_type=jnp.float32)
    hidden = lax.psum(partial_hidden, "row")
    activation = gelu_exact(hidden).astype(jnp.bfloat16)
    segment = activation
    output = lax.psum_scatter(
        jnp.dot(segment, w_out, preferred_element_type=jnp.float32),
        "col",
        scatter_dimension=0,
        tiled=True,
    )
    cotangent = lax.all_gather(d_output, "col", axis=0, tiled=True)
    grad_w_out = lax.dot_general(
        activation, cotangent, (((0,), (0,)), ((), ())), preferred_element_type=jnp.float32
    )
    back_grad = lax.dot_general(
        cotangent, w_out, (((1,), (1,)), ((), ())), preferred_element_type=jnp.float32
    )
    grad_whole = lax.psum(back_grad, "row")
    hidden_grad = (grad_whole * gelu_slope(hidden)).astype(jnp.bfloat16)
    grad_w_in = lax.dot_general(
        gathered, hidden_grad, (((0,), (0,)), ((), ())), preferred_element_type=jnp.float32
    )
    segment = hidden_grad
    grad_tokens = lax.psum_scatter(
        lax.dot_general(
            segment, w_in, (((1,), (1,)), ((), ())), preferred_element_type=jnp.float32
        ),
        "col",
        scatter_dimension=0,
        tiled=True,
    )
    return (output, grad_tokens, grad_w_in, grad_w_out)


def solution(mesh):
    placed = (P("col", "row"), P("row", "col"), P("col", "row"), P("col", "row"))
    return jax.shard_map(
        shards,
        mesh=mesh,
        in_specs=placed,
        out_specs=(P("col", "row"), P("col", "row"), P("row", "col"), P("col", "row")),
        check_vma=False,
    )
```

profile of v0, /device:TPU:1, one launch (start us, length us, event | category | flops | bytes accessed | tf_op | source)
XLA Modules:
  0.0 403.2 jit_solution(6003368156919888161)
XLA Ops:
  7.2 0.0 copy-start
  7.2 0.0 all-reduce.3.cloned.1.call-start
  7.2 20.4 %all_gather.6 = bf16[1024,384]{1,0:T(8,128)(2,1)S(1)} all-gather(bf16[64,384]{1,0:T(8,128)(2,1)} %param.4), channel_id=1, replica_groups=mesh['row'=16,'col'=16] {'col'}, dimensions={0}, use_global_device_ids=true | all-gather | bytes 835584 | tf_op jit(solution)/shard_map/all_gather | solution.py:17
  27.7 18.3 %all_gather.7 = bf16[1024,384]{1,0:T(8,128)(2,1)S(1)} all-gather(bf16[64,384]{1,0:T(8,128)(2,1)} %param.7), channel_id=1, replica_groups=mesh['row'=16,'col'=16] {'col'}, dimensions={0}, use_global_device_ids=true | all-gather | bytes 835584 | tf_op jit(solution)/shard_map/all_gather | solution.py:28
  46.0 5.7 %fusion.8 = f32[1024,1536]{1,0:T(8,128)} fusion(bf16[1024,384]{1,0:T(8,128)(2,1)S(1)} %all_gather.7, bf16[1536,384]{1,0:T(8,128)(2,1)} %param.6), kind=kOutput, calls=%fused_computation.12 | convolution fusion | flops 1207959552 | bytes 8257536 | tf_op jit(solution)/shard_map/dot_general | solution.py:32
  51.7 0.0 copy-done
  51.7 4.4 %fusion.6 = f32[1024,1536]{1,0:T(8,128)} fusion(bf16[1024,384]{1,0:T(8,128)(2,1)S(1)} %all_gather.6, bf16[384,1536]{1,0:T(8,128)(2,1)S(1)} %copy-done), kind=kOutput, calls=%fused_computation.10 | convolution fusion | flops 1207959552 | bytes 8257536 | tf_op jit(solution)/shard_map/dot_general | solution.py:18
  56.0 0.0 all-reduce.3.cloned.1.call-update
  56.1 0.0 reduce-scatter.5.cloned.1.call-start
  56.1 168.6 %all-reduce.3.cloned.1.call-done = (f32[1024,1536]{1,0:T(8,128)}, f32[1024,1536]{1,0:T(8,128)}) async-done(((f32[1024,1536]{1,0:T(8,128)}, f32[1024,1536]{1,0:T(8,128)}), (f32[1024,1536]{1,0:T(8,128)}, f32[1024,1536]{1,0:T(8,128)})) %all-reduce.3.cloned.1.call-update) | async-done | bytes 12582928 | tf_op jit(solution)/shard_map/psum | solution.py:19
  224.7 8.4 %fusion.5 = (bf16[1024,1536]{1,0:T(8,128)(2,1)S(1)}, bf16[1024,1536]{1,0:T(8,128)(2,1)}) fusion(f32[1024,1536]{1,0:T(8,128)} %get-tuple-element.9, f32[1024,1536]{1,0:T(8,128)} %get-tuple-element.8), kind=kLoop, calls=%fused_computation.6 | loop fusion | flops 20447232 | bytes 18874368 | tf_op jit(solution)/shard_map/convert_element_type | solution.py:36
  233.1 0.0 copy-start.1
  233.1 1.7 copy-done.1
  234.8 3.0 fusion.9
  237.7 0.0 reduce-scatter.5.cloned.1.call-update
  237.8 0.0 reduce-scatter.3.cloned.1.call-start
  237.8 5.2 %fusion.7 = f32[1024,384]{1,0:T(8,128)} fusion(bf16[1024,1536]{1,0:T(8,128)(2,1)} %get-tuple-element.11, bf16[1536,384]{1,0:T(8,128)(2,1)} %param.6), kind=kOutput, calls=%fused_computation.11 | convolution fusion | flops 1207959552 | bytes 5898240 | tf_op jit(solution)/shard_map/dot_general | solution.py:23
  243.0 0.0 reduce-scatter.3.cloned.1.call-update
  243.0 5.1 %convolution_bitcast_fusion = f32[384,1536]{0,1:T(8,128)} fusion(bf16[1024,1536]{1,0:T(8,128)(2,1)} %copy-done.1, bf16[1024,384]{1,0:T(8,128)(2,1)S(1)} %all_gather.6), kind=kOutput, calls=%fused_computation.9 | convolution fusion | flops 1207959552 | bytes 6291456 | tf_op jit(solution)/shard_map/dot_general | solution.py:37
  248.1 3.0 copy.8
  251.2 5.1 %fusion.10 = f32[1536,384]{1,0:T(8,128)} fusion(bf16[1024,1536]{1,0:T(8,128)(2,1)} %get-tuple-element.11, bf16[1024,384]{1,0:T(8,128)(2,1)S(1)} %all_gather.7), kind=kOutput, calls=%fused_computation.14 | convolution fusion | flops 1207959552 | bytes 6291456 | tf_op jit(solution)/shard_map/dot_general | solution.py:29
  256.3 58.3 %reduce-scatter.5.cloned.1.call-done = f32[64,384]{1,0:T(8,128)} async-done(((f32[1024,384]{1,0:T(8,128)}), f32[64,384]{1,0:T(8,128)}) %reduce-scatter.5.cloned.1.call-update) | async-done | bytes 98320 | tf_op jit(solution)/shard_map/reduce_scatter | solution.py:41
  314.6 82.1 %reduce-scatter.3.cloned.1.call-done = f32[64,384]{1,0:T(8,128)} async-done(((f32[1024,384]{1,0:T(8,128)}), f32[64,384]{1,0:T(8,128)}) %reduce-scatter.3.cloned.1.call-update) | async-done | bytes 98320 | tf_op jit(solution)/shard_map/reduce_scatter | solution.py:22
Async XLA Ops:
  7.2 44.5 %copy-start = (bf16[384,1536]{1,0:T(8,128)(2,1)S(1)}, bf16[384,1536]{1,0:T(8,128)(2,1)}, u32[]{:S(2)}) copy-start(bf16[384,1536]{1,0:T(8,128)(2,1)} %param.5) | copy-start | bytes 3538948
  7.2 217.5 %all-reduce.3.cloned.1.call-start = ((), (), s32[]{:S(2)}) async-start(), calls=%async_computation.4 | async-start | bytes 25165824 | tf_op jit(solution)/shard_map/psum | solution.py:19
  56.1 258.5 %reduce-scatter.5.cloned.1.call-start = ((), (), s32[]{:S(2)}) async-start(), calls=%async_computation.3 | async-start | bytes 1671168 | tf_op jit(solution)/shard_map/reduce_scatter | solution.py:41
  233.1 1.7 copy-start.1
  237.8 158.9 %reduce-scatter.3.cloned.1.call-start = ((), (), s32[]{:S(2)}) async-start(), calls=%async_computation.2 | async-start | bytes 1671168 | tf_op jit(solution)/shard_map/reduce_scatter | solution.py:22
Sparse Core Ops, SparseCore 0:
  56.2 168.4 all-reduce.2
  237.9 76.6 reduce-scatter.4
  318.7 77.9 reduce-scatter.2
where the time goes:
time: 404 us; the launch traced here: 403 us
  waiting for transfers between devices  309 us (76%)
  blocking collectives  38.7 us (10%)
  matrix products  28.5 us (7%)
  between operations  13.8 us (3%)
  other arithmetic  8.4 us (2%)
  local copies, waits for them, and re-layouts  4.71 us (1%)
    psum x1, waiting for transfers between devices, shards(): hidden = lax.psum(partial_hidden, 'row')  169 us
    reduce_scatter x1, waiting for transfers between devices, shards(): lax.psum_scatter(jnp.dot(segment, w_out, preferred_element_type=jnp.float...  82.1 us
    reduce_scatter x1, waiting for transfers between devices, shards(): lax.psum_scatter(lax.dot_general(segment, w_in, (((1,), (1,)), ((), ())),...  58.3 us
    all_gather x1, blocking collectives, shards(): gathered = lax.all_gather(tokens, 'col', axis=0, tiled=True)  20.4 us
    all_gather x1, blocking collectives, shards(): cotangent = lax.all_gather(d_output, 'col', axis=0, tiled=True)  18.3 us
    convert_element_type x1, other arithmetic, shards(): hidden_grad = (grad_whole * gelu_slope(hidden)).astype(jnp.bfloat16)  8.4 us
  transfers between devices with their start and end apart: 3, of which 3 were waited for; matrix products, arithmetic and copies ran while one was open for 5% of the time, Pallas kernels for 0%

commit v1 on v0

v1 whole, which is shorter than its diff:
```python
import functools

import jax
import jax.numpy as jnp
from jax import lax
from jax.experimental import pallas as pl
from jax.experimental.pallas import tpu as pltpu
from jax.sharding import PartitionSpec as P

F32, BF16 = jnp.float32, jnp.bfloat16
MESH = pl.DeviceIdType.MESH
NZ = 8
BLK = 64
WID = 384
HID = 1536
HALF = 768
NCH = 4
CHR = 256
RZ = CHR // NZ
SUM_SCALE = 2.0**19
OUT_SCALE = 2.0**9

OFFS = [
    (0, 0), (0, 1), (0, 3), (0, 2),
    (2, 2), (2, 1), (2, 3), (1, 2),
    (3, 2), (3, 1), (3, 3), (1, 3),
    (1, 1), (2, 0), (3, 0), (1, 0),
]


def gelu_exact(values):
    return values * 0.5 * (1.0 + lax.erf(values * 0.7071067811865476))


def gelu_slope(values):
    normal_cdf = 0.5 * (1.0 + lax.erf(values * 0.7071067811865476))
    return normal_cdf + values * jnp.exp(-0.5 * values * values) * 0.3989422804014327


def enc(v):
    return ((v * jnp.abs(v)) * (v * v)).astype(BF16)


def dec(code):
    y = code.astype(F32)
    root = lax.rsqrt(lax.rsqrt(jnp.abs(y)))
    return jnp.where(y == 0.0, 0.0, jnp.where(y < 0.0, -root, root))


def kernel(
    tok_ref, win_ref, wout_ref, dout_ref,
    out_ref, gt_ref, gwi_ref, gwo_ref,
    acts, xs, wc0, wc1, part, snd, rcv, hid, osnd, orcv, osum,
    loc_sem, tok_s, tok_r, fwd_s, fwd_r, w_s, w_r,
    rs_s, rs_r, ag_s, ag_r, sib_s, sib_r, out_s, out_r,
):
    row = lax.axis_index("row")
    col = lax.axis_index("col")
    z, core = row // 2, row % 2
    x, y = col // 4, col % 4
    other = 1 - core
    sib = (z * 2 + other, col)
    z_to = [(((z + 1) % NZ) * 2 + core, col), (((z + NZ - 1) % NZ) * 2 + core, col)]

    def shift(by):
        return (z + by + NZ) % NZ

    def peer(dx, dy):
        return (row, ((x + dx + 4) % 4) * 4 + (y + dy + 4) % 4)

    own_w = pl.ds(pl.multiple_of(core * WID, WID), WID)
    own_h = pl.ds(pl.multiple_of(core * HALF, HALF), HALF)
    oth_h = pl.ds(pl.multiple_of(other * HALF, HALF), HALF)
    halves = [pl.ds(0, WID), pl.ds(WID, WID)]
    x_in = [tok_ref, dout_ref]

    def remote(src, dst, s, r, dev):
        return pltpu.make_async_remote_copy(
            src_ref=src, dst_ref=dst, send_sem=s, recv_sem=r, device_id=dev, device_id_type=MESH
        )

    barrier = pltpu.get_barrier_semaphore()
    greeted = [sib, *z_to] + [peer(dx, dy) for dx, dy in OFFS[1:]]
    for dev in greeted:
        pl.semaphore_signal(barrier, inc=1, device_id=dev, device_id_type=MESH)
    local = [
        pltpu.make_async_copy(tok_ref, xs.at[0, pl.ds(0, BLK), own_w], loc_sem.at[0]),
        pltpu.make_async_copy(dout_ref, xs.at[1, pl.ds(0, BLK), own_w], loc_sem.at[1]),
        pltpu.make_async_copy(win_ref.at[:, own_h], wc0.at[own_w, :], loc_sem.at[2]),
        pltpu.make_async_copy(wout_ref.at[own_h, :], wc1.at[:, own_w], loc_sem.at[3]),
    ]
    for c in local:
        c.start()
    pl.semaphore_wait(barrier, len(greeted))

    def tok_copy(t, p):
        dx, dy = OFFS[p]
        return remote(
            x_in[t], xs.at[t, pl.ds(p * BLK, BLK), own_w], tok_s.at[t, p], tok_r.at[t, p], peer(-dx, -dy)
        )

    def fwd_copy(t, k):
        place = xs.at[t, pl.ds(k * CHR, CHR), own_w]
        return remote(place, place, fwd_s.at[t, k], fwd_r.at[t, k], sib)

    w_copies = [
        remote(win_ref.at[:, oth_h], wc0.at[own_w, :], w_s.at[0], w_r.at[0], sib),
        remote(wout_ref.at[oth_h, :], wc1.at[:, own_w], w_s.at[1], w_r.at[1], sib),
    ]

    for t in range(2):
        for p in range(1, 4):
            tok_copy(t, p).start()
        w_copies[t].start()
    for c in local:
        c.wait()
    for p in range(4, 16):
        for t in range(2):
            tok_copy(t, p).start()

    def arrive(t, k):
        for p in range(4 * k, 4 * k + 4):
            if p:
                tok_copy(t, p).wait_recv()
        fwd_copy(t, k).start()

    def partial(t, k):
        fwd_copy(t, k).wait_recv()
        rows = pl.ds(k * CHR, CHR)

        def tile(n, carry):
            cols = pl.ds(pl.multiple_of(n * 256, 256), 256)
            if t == 0:
                got = jnp.dot(xs[0, rows, :], wc0[:, cols], preferred_element_type=F32)
            else:
                got = lax.dot_general(
                    xs[1, rows, :], wc1[cols, :], (((1,), (1,)), ((), ())), preferred_element_type=F32
                )
            part[t, k, :, cols] = got * SUM_SCALE
            return carry

        lax.fori_loop(0, HALF // 256, tile, 0)

    def rs_copy(t, k, d, r):
        at = (t, k, d, r)
        if r == 0:
            src, dst = snd.at[t, k, d, r, :, halves[d]], rcv.at[t, k, d, r, :, halves[d]]
        else:
            src, dst = snd.at[at], rcv.at[at]
        return remote(src, dst, rs_s.at[at], rs_r.at[at], z_to[d])

    def rs_one(t, k, r):
        for d in range(2):
            owner = shift(4 - r if d == 0 else r - 4)
            rows = pl.ds(pl.multiple_of(owner * RZ, RZ), RZ)
            mine = halves[d]
            if r == 0:
                snd[t, k, d, r, :, mine] = enc(part[t, k, rows, mine])
            else:
                rs_copy(t, k, d, r - 1).wait_recv()
                if r == 1:
                    rest = halves[1 - d]
                    snd[t, k, d, r, :, mine] = enc(dec(rcv[t, k, d, 0, :, mine]) + part[t, k, rows, mine])
                    snd[t, k, d, r, :, rest] = enc(part[t, k, rows, rest])
                else:
                    snd[t, k, d, r] = enc(dec(rcv[t, k, d, r - 1]) + part[t, k, rows, :])
            rs_copy(t, k, d, r).start()

    def both(fn):
        def body(t, carry):
            fn(t)
            return carry

        lax.fori_loop(0, 2, body, 0)

    def rs(k, r):
        both(lambda t: rs_one(t, k, r))

    def ag_copy(t, k, d, r, b):
        rows = pl.ds(pl.multiple_of(k * CHR + b * RZ, RZ), RZ)
        if r == 3:
            cols = pl.ds(pl.multiple_of(core * HALF + d * WID, WID), WID)
        else:
            cols = own_h
        place = acts.at[t, rows, cols]
        return remote(place, place, ag_s.at[t, k, d, r], ag_r.at[t, k, d, r], z_to[d])

    def ag_wait(t, k, d, r):
        ag_copy(t, k, d, r, shift(-(r + 1) if d == 0 else r + 1)).wait_recv()

    def ag_one(t, k, r):
        for d in range(2):
            if r:
                ag_wait(t, k, d, r - 1)
            ag_copy(t, k, d, r, shift(-r if d == 0 else r)).start()

    def ag(k, r):
        both(lambda t: ag_one(t, k, r))

    def settle(k):
        rows = pl.ds(pl.multiple_of(z * RZ, RZ), RZ)
        place = pl.ds(pl.multiple_of(k * CHR + z * RZ, RZ), RZ)
        for t in range(2):
            for d in range(2):
                rs_copy(t, k, d, 3).wait_recv()
            total = (dec(rcv[t, k, 0, 3]) + dec(rcv[t, k, 1, 3]) + part[t, k, rows, :]) * (1.0 / SUM_SCALE)
            if t == 0:
                hid[...] = total
                acts[0, place, own_h] = gelu_exact(total).astype(BF16)
            else:
                acts[1, place, own_h] = (total * gelu_slope(hid[...])).astype(BF16)
            ag_one(t, k, 0)

    def sib_copy(t, k):
        place = acts.at[t, pl.ds(k * CHR, CHR), own_h]
        return remote(place, place, sib_s.at[t, k], sib_r.at[t, k], sib)

    def gathered(k):
        for t in range(2):
            for d in range(2):
                ag_wait(t, k, d, 3)
            sib_copy(t, k).start()

    def out_copy(t, p):
        return remote(osnd.at[t, p], orcv.at[t, p], out_s.at[t, p], out_r.at[t, p], peer(*OFFS[p]))

    def project(k):
        rows = pl.ds(k * CHR, CHR)
        for t in range(2):
            sib_copy(t, k).wait_recv()
            if t == 0:
                got = jnp.dot(acts[0, rows, :], wout_ref[...], preferred_element_type=F32)
            else:
                got = lax.dot_general(
                    acts[1, rows, :], win_ref[...], (((1,), (1,)), ((), ())), preferred_element_type=F32
                )
            got = got * OUT_SCALE
            for i in range(4):
                p = 4 * k + i
                block = got[i * BLK : (i + 1) * BLK, :]
                if p == 0:
                    osum[t] = block
                else:
                    osnd[t, p] = enc(block)
                    out_copy(t, p).start()

    def weight_grads(k):
        rows = pl.ds(k * CHR, CHR)

        def tile(n, carry):
            cols = pl.ds(pl.multiple_of(n * 256, 256), 256)
            more = lax.dot_general(
                acts[0, rows, cols], xs[1, rows, own_w], (((0,), (0,)), ((), ())), preferred_element_type=F32
            )
            gwo_ref[cols, :] = more if k == 0 else gwo_ref[cols, :] + more
            more = lax.dot_general(
                xs[0, rows, own_w], acts[1, rows, cols], (((0,), (0,)), ((), ())), preferred_element_type=F32
            )
            gwi_ref[:, cols] = more if k == 0 else gwi_ref[:, cols] + more
            return carry

        lax.fori_loop(0, HID // 256, tile, 0)

    arrive(0, 0)
    w_copies[0].wait_recv()
    partial(0, 0)
    rs_one(0, 0, 0)
    arrive(1, 0)
    w_copies[1].wait_recv()
    partial(1, 0)
    rs_one(1, 0, 0)
    for t in range(2):
        arrive(t, 1)
    for t in range(2):
        partial(t, 1)
    rs(0, 1); rs(1, 0)
    for t in range(2):
        arrive(t, 2)
    rs(0, 2); rs(1, 1)
    for t in range(2):
        partial(t, 2)
        arrive(t, 3)
    rs(0, 3); rs(1, 2)
    for t in range(2):
        partial(t, 3)
    settle(0); rs(1, 3); rs(2, 0)
    ag(0, 1); settle(1); rs(2, 1); rs(3, 0)
    ag(0, 2); ag(1, 1); rs(2, 2); rs(3, 1)
    ag(0, 3); ag(1, 2); rs(2, 3); rs(3, 2)
    gathered(0); ag(1, 3); settle(2); rs(3, 3)
    project(0)
    gathered(1); ag(2, 1); settle(3)
    weight_grads(0)
    ag(2, 2); ag(3, 1)
    project(1)
    weight_grads(1)
    ag(2, 3); ag(3, 2)
    gathered(2); ag(3, 3)
    project(2)
    weight_grads(2)
    gathered(3)
    project(3)
    weight_grads(3)

    for t in range(2):
        def add(p, carry, t=t):
            out = remote(osnd.at[t, p], orcv.at[t, p], out_s.at[t, p], out_r.at[t, p], sib)
            out.wait_recv()
            osum[t] = osum[t] + dec(orcv[t, p])
            return carry

        lax.fori_loop(1, 16, add, 0)
    out_ref[...] = osum[0] * (1.0 / OUT_SCALE)
    gt_ref[...] = osum[1] * (1.0 / OUT_SCALE)

    for t in range(2):
        w_copies[t].wait_send()
        for p in range(1, 16):
            tok_copy(t, p).wait_send()
            out_copy(t, p).wait_send()
        for k in range(NCH):
            fwd_copy(t, k).wait_send()
            sib_copy(t, k).wait_send()
            for d in range(2):
                for r in range(4):
                    rs_copy(t, k, d, r).wait_send()
                    ag_copy(t, k, d, r, shift(-r if d == 0 else r)).wait_send()


def shards(tokens, w_in, w_out, d_output):
    vmem = pl.BlockSpec(memory_space=pltpu.VMEM)
    dma = pltpu.SemaphoreType.DMA
    return pl.pallas_call(
        kernel,
        out_shape=(
            jax.ShapeDtypeStruct((BLK, WID), F32),
            jax.ShapeDtypeStruct((BLK, WID), F32),
            jax.ShapeDtypeStruct((WID, HID), F32),
            jax.ShapeDtypeStruct((HID, WID), F32),
        ),
        in_specs=[vmem] * 4,
        out_specs=(vmem,) * 4,
        scratch_shapes=[
            pltpu.VMEM((2, NCH * CHR, HID), BF16),
            pltpu.VMEM((2, NCH * CHR, HALF), BF16),
            pltpu.VMEM((HALF, HALF), BF16),
            pltpu.VMEM((HALF, HALF), BF16),
            pltpu.VMEM((2, NCH, CHR, HALF), F32),
            pltpu.VMEM((2, NCH, 2, 4, RZ, HALF), BF16),
            pltpu.VMEM((2, NCH, 2, 4, RZ, HALF), BF16),
            pltpu.VMEM((RZ, HALF), F32),
            pltpu.VMEM((2, 16, BLK, WID), BF16),
            pltpu.VMEM((2, 16, BLK, WID), BF16),
            pltpu.VMEM((2, BLK, WID), F32),
            dma((4,)),
            dma((2, 16)), dma((2, 16)),
            dma((2, NCH)), dma((2, NCH)),
            dma((2,)), dma((2,)),
            dma((2, NCH, 2, 4)), dma((2, NCH, 2, 4)),
            dma((2, NCH, 2, 4)), dma((2, NCH, 2, 4)),
            dma((2, NCH)), dma((2, NCH)),
            dma((2, 16)), dma((2, 16)),
        ],
        compiler_params=pltpu.CompilerParams(
            collective_id=0, has_side_effects=True, vmem_limit_bytes=56 * 2**20
        ),
    )(tokens, w_in, w_out, d_output)


def solution(mesh):
    placed = (P("col", "row"), P("row", "col"), P("col", "row"), P("col", "row"))
    return jax.shard_map(
        shards,
        mesh=mesh,
        in_specs=placed,
        out_specs=(P("col", "row"), P("col", "row"), P("row", "col"), P("col", "row")),
        check_vma=False,
    )
```

time: 404 us -> 129 us (0.32)
  waiting for transfers between devices: 309 us -> 0 us
  Pallas kernels: 0 us -> 121 us
  blocking collectives: 38.7 us -> 0 us
  matrix products: 28.5 us -> 0 us
  between operations: 13.8 us -> 0.64 us
  other arithmetic: 8.4 us -> 0 us
    psum x1 -> x0, waiting for transfers between devices: 169 us -> none  [shards(): hidden = lax.psum(partial_hidden, 'row')]
    reduce_scatter x2 -> x0, waiting for transfers between devices: 140 us -> none  [the longest x1 82.1 us: shards(): lax.psum_scatter(jnp.dot(segment, w_out, preferred_element_type=jnp.float...]
    pallas_call x0 -> x1, Pallas kernels: none -> 121 us  [shards(): pl.pallas_call(kernel, out_shape=(jax.ShapeDtypeStruct((BLK, WID), F32),...]
    all_gather x2 -> x0, blocking collectives: 38.7 us -> none  [the longest x1 20.4 us: shards(): gathered = lax.all_gather(tokens, 'col', axis=0, tiled=True)]
    dot_general x6 -> x0, matrix products: 28.5 us -> none  [the longest x1 5.7 us: shards(): lax.dot_general(cotangent, w_out, (((1,), (1,)), ((), ())), preferred_ele...]
    convert_element_type x1 -> x0, other arithmetic: 8.4 us -> none  [shards(): hidden_grad = (grad_whole * gelu_slope(hidden)).astype(jnp.bfloat16)]
  transfers between devices with their start and end apart: 3 -> 0, of which waited for: 3 -> 0; matrix products, arithmetic and copies ran while one was open for 5% -> 0% of each run, Pallas kernels for 0% -> 0%
where the time goes in v1:
time: 129 us
  Pallas kernels  121 us (94%)
  local copies, waits for them, and re-layouts  7.86 us (6%)
    pallas_call x1, Pallas kernels, shards(): pl.pallas_call(kernel, out_shape=(jax.ShapeDtypeStruct((BLK, WID), F32),...  121 us
    unnamed x6, local copies, waits for them, and re-layouts  7.86 us

profile of v1, /device:TPU:1, one launch (start us, length us, event | category | flops | bytes accessed | tf_op | source)
XLA Modules:
  0.0 129.2 jit_solution(13692836871018076570)
XLA Ops:
  0.6 120.7 %shard_map.75 = (f32[64,384]{1,0:T(8,128)}, f32[64,384]{1,0:T(8,128)}, f32[384,1536]{1,0:T(8,128)}, f32[1536,384]{1,0:T(8,128)}) custom-call(bf16[64,384]{1,0:T(8,128)(2,1)} %tok_ref.1, bf16[384,1536]{1,0:T(8,128)(2,1)} %win_ref.1, bf16[1536,384]{1,0:T(8,128)(2,1)} %wout_ref.1, bf16[64,384]{1,0:T(8,128)(2,1)} %dout_ref.1), custom_call_target="tpu_custom_call" | custom-call | tf_op jit(solution)/shard_map/pallas_call | solution.py:333
  121.3 1.5 %copy.12 = f32[64,384]{1,0:T(8,128)} copy(f32[64,384]{1,0:T(8,128)} %get-tuple-element.8) | data formatting | bytes 196608
  122.9 1.5 %copy.13 = f32[64,384]{1,0:T(8,128)} copy(f32[64,384]{1,0:T(8,128)} %get-tuple-element.9) | data formatting | bytes 196608
  124.4 0.0 copy-start
  124.4 3.4 %copy.14 = f32[384,1536]{1,0:T(8,128)} copy(f32[384,1536]{1,0:T(8,128)} %get-tuple-element.10) | data formatting | bytes 4718592
  127.8 0.0 copy-done
  127.8 1.4 %copy.15 = f32[1536,384]{1,0:T(8,128)} copy(f32[1536,384]{1,0:T(8,128)S(1)} %copy-done) | data formatting | bytes 4718592
Async XLA Ops:
  124.4 3.4 %copy-start = (f32[1536,384]{1,0:T(8,128)S(1)}, f32[1536,384]{1,0:T(8,128)}, u32[]{:S(2)}) copy-start(f32[1536,384]{1,0:T(8,128)} %get-tuple-element.11) | copy-start | bytes 7077892

commit v2 on v1

--- a/solution.py
+++ b/solution.py
@@ -20,12 +20,9 @@
 SUM_SCALE = 2.0**19
 OUT_SCALE = 2.0**9
 
-OFFS = [
-    (0, 0), (0, 1), (0, 3), (0, 2),
-    (2, 2), (2, 1), (2, 3), (1, 2),
-    (3, 2), (3, 1), (3, 3), (1, 3),
-    (1, 1), (2, 0), (3, 0), (1, 0),
-]
+STEPS = [0, 1, 3, 2]
+PART = CHR // 2
+SUB = BLK // 2
 
 
 def gelu_exact(values):
@@ -48,11 +45,11 @@
 
 
 def kernel(
-    tok_ref, win_ref, wout_ref, dout_ref,
+    tok_ref, win_hbm, wout_hbm, dout_ref,
     out_ref, gt_ref, gwi_ref, gwo_ref,
-    acts, xs, wc0, wc1, part, snd, rcv, hid, osnd, orcv, osum,
-    loc_sem, tok_s, tok_r, fwd_s, fwd_r, w_s, w_r,
-    rs_s, rs_r, ag_s, ag_r, sib_s, sib_r, out_s, out_r,
+    win_ref, wout_ref, acts, xs, wc0, wc1, part, snd, rcv, hid, osnd, orcv, osum,
+    loc_sem, one_s, one_r, two_s, two_r, fwd_s, fwd_r, w_s, w_r,
+    rs_s, rs_r, ag_s, ag_r, sib_s, sib_r, last_s, last_r, out_s, out_r,
 ):
     row = lax.axis_index("row")
     col = lax.axis_index("col")
@@ -80,23 +77,40 @@
         )
 
     barrier = pltpu.get_barrier_semaphore()
-    greeted = [sib, *z_to] + [peer(dx, dy) for dx, dy in OFFS[1:]]
+    greeted = [sib, *z_to] + [peer(dx, dy) for dx in range(4) for dy in range(4) if dx or dy]
     for dev in greeted:
         pl.semaphore_signal(barrier, inc=1, device_id=dev, device_id_type=MESH)
     local = [
-        pltpu.make_async_copy(tok_ref, xs.at[0, pl.ds(0, BLK), own_w], loc_sem.at[0]),
-        pltpu.make_async_copy(dout_ref, xs.at[1, pl.ds(0, BLK), own_w], loc_sem.at[1]),
-        pltpu.make_async_copy(win_ref.at[:, own_h], wc0.at[own_w, :], loc_sem.at[2]),
-        pltpu.make_async_copy(wout_ref.at[own_h, :], wc1.at[:, own_w], loc_sem.at[3]),
+        pltpu.make_async_copy(
+            x_in[t].at[pl.ds(ab * SUB, SUB), :], xs.at[t, pl.ds(ab * PART, SUB), own_w], loc_sem.at[t * 2 + ab]
+        )
+        for t in range(2)
+        for ab in range(2)
+    ]
+    local += [
+        pltpu.make_async_copy(win_hbm.at[:, own_h], wc0.at[own_w, :], loc_sem.at[4]),
+        pltpu.make_async_copy(wout_hbm.at[own_h, :], wc1.at[:, own_w], loc_sem.at[5]),
+        pltpu.make_async_copy(win_hbm, win_ref, loc_sem.at[6]),
+        pltpu.make_async_copy(wout_hbm, wout_ref, loc_sem.at[7]),
     ]
     for c in local:
         c.start()
     pl.semaphore_wait(barrier, len(greeted))
 
-    def tok_copy(t, p):
-        dx, dy = OFFS[p]
+    def one_copy(t, ab, i):
+        to = peer(0, -STEPS[i]) if ab == 0 else peer(-STEPS[i], 0)
         return remote(
-            x_in[t], xs.at[t, pl.ds(p * BLK, BLK), own_w], tok_s.at[t, p], tok_r.at[t, p], peer(-dx, -dy)
+            x_in[t].at[pl.ds(ab * SUB, SUB), :],
+            xs.at[t, pl.ds(ab * PART + i * SUB, SUB), own_w],
+            one_s.at[t, ab, i], one_r.at[t, ab, i], to,
+        )
+
+    def two_copy(t, ab, j):
+        to = peer(-STEPS[j], 0) if ab == 0 else peer(0, -STEPS[j])
+        return remote(
+            xs.at[t, pl.ds(ab * PART, PART), own_w],
+            xs.at[t, pl.ds(j * CHR + ab * PART, PART), own_w],
+            two_s.at[t, ab, j], two_r.at[t, ab, j], to,
         )
 
     def fwd_copy(t, k):
@@ -104,24 +118,22 @@
         return remote(place, place, fwd_s.at[t, k], fwd_r.at[t, k], sib)
 
     w_copies = [
-        remote(win_ref.at[:, oth_h], wc0.at[own_w, :], w_s.at[0], w_r.at[0], sib),
-        remote(wout_ref.at[oth_h, :], wc1.at[:, own_w], w_s.at[1], w_r.at[1], sib),
+        remote(win_hbm.at[:, oth_h], wc0.at[own_w, :], w_s.at[0], w_r.at[0], sib),
+        remote(wout_hbm.at[oth_h, :], wc1.at[:, own_w], w_s.at[1], w_r.at[1], sib),
     ]
 
-    for t in range(2):
-        for p in range(1, 4):
-            tok_copy(t, p).start()
-        w_copies[t].start()
-    for c in local:
-        c.wait()
-    for p in range(4, 16):
-        for t in range(2):
-            tok_copy(t, p).start()
+    def spread(t, j):
+        for ab in range(2):
+            two_copy(t, ab, j).start()
 
     def arrive(t, k):
-        for p in range(4 * k, 4 * k + 4):
-            if p:
-                tok_copy(t, p).wait_recv()
+        for ab in range(2):
+            if k:
+                two_copy(t, ab, k).wait_recv()
+            else:
+                local[t * 2 + ab].wait()
+                for i in range(1, 4):
+                    one_copy(t, ab, i).wait_recv()
         fwd_copy(t, k).start()
 
     def partial(t, k):
@@ -192,7 +204,10 @@
         for d in range(2):
             if r:
                 ag_wait(t, k, d, r - 1)
-            ag_copy(t, k, d, r, shift(-r if d == 0 else r)).start()
+            block = shift(-r if d == 0 else r)
+            ag_copy(t, k, d, r, block).start()
+            if k == NCH - 1 and (r or d == 0):
+                last_copy(t, d * 3 + r, block).start()
 
     def ag(k, r):
         both(lambda t: ag_one(t, k, r))
@@ -215,19 +230,36 @@
         place = acts.at[t, pl.ds(k * CHR, CHR), own_h]
         return remote(place, place, sib_s.at[t, k], sib_r.at[t, k], sib)
 
+    def last_copy(t, i, block):
+        rows = pl.ds(pl.multiple_of((NCH - 1) * CHR + block * RZ, RZ), RZ)
+        place = acts.at[t, rows, own_h]
+        return remote(place, place, last_s.at[t, i], last_r.at[t, i], sib)
+
+    def last_block(i):
+        return shift(-i if i < 4 else i - 3) if i < 7 else shift(4)
+
     def gathered(k):
         for t in range(2):
             for d in range(2):
                 ag_wait(t, k, d, 3)
-            sib_copy(t, k).start()
-
-    def out_copy(t, p):
-        return remote(osnd.at[t, p], orcv.at[t, p], out_s.at[t, p], out_r.at[t, p], peer(*OFFS[p]))
+            if k == NCH - 1:
+                last_copy(t, 7, shift(4)).start()
+            else:
+                sib_copy(t, k).start()
+
+    def out_copy(t, ab, n):
+        near, far = STEPS[n // 4], STEPS[n % 4]
+        to = peer(near, far) if ab == 0 else peer(far, near)
+        return remote(osnd.at[t, ab, n], orcv.at[t, ab, n], out_s.at[t, ab, n], out_r.at[t, ab, n], to)
 
     def project(k):
         rows = pl.ds(k * CHR, CHR)
         for t in range(2):
-            sib_copy(t, k).wait_recv()
+            if k == NCH - 1:
+                for i in range(8):
+                    last_copy(t, i, last_block(i)).wait_recv()
+            else:
+                sib_copy(t, k).wait_recv()
             if t == 0:
                 got = jnp.dot(acts[0, rows, :], wout_ref[...], preferred_element_type=F32)
             else:
@@ -235,14 +267,15 @@
                     acts[1, rows, :], win_ref[...], (((1,), (1,)), ((), ())), preferred_element_type=F32
                 )
             got = got * OUT_SCALE
-            for i in range(4):
-                p = 4 * k + i
-                block = got[i * BLK : (i + 1) * BLK, :]
-                if p == 0:
-                    osum[t] = block
-                else:
-                    osnd[t, p] = enc(block)
-                    out_copy(t, p).start()
+            for ab in range(2):
+                for i in range(4):
+                    n = 4 * k + i
+                    block = got[ab * PART + i * SUB : ab * PART + (i + 1) * SUB, :]
+                    if n == 0:
+                        osum[t, pl.ds(ab * SUB, SUB), :] = block
+                    else:
+                        osnd[t, ab, n] = enc(block)
+                        out_copy(t, ab, n).start()
 
     def weight_grads(k):
         rows = pl.ds(k * CHR, CHR)
@@ -261,14 +294,22 @@
 
         lax.fori_loop(0, HID // 256, tile, 0)
 
-    arrive(0, 0)
-    w_copies[0].wait_recv()
-    partial(0, 0)
-    rs_one(0, 0, 0)
-    arrive(1, 0)
-    w_copies[1].wait_recv()
-    partial(1, 0)
-    rs_one(1, 0, 0)
+    for t in range(2):
+        for i in range(1, 4):
+            for ab in range(2):
+                one_copy(t, ab, i).start()
+        w_copies[t].start()
+    for t in range(2):
+        arrive(t, 0)
+        spread(t, 1)
+    for t in range(2):
+        local[4 + t].wait()
+        w_copies[t].wait_recv()
+        partial(t, 0)
+        rs_one(t, 0, 0)
+    for j in range(2, NCH):
+        for t in range(2):
+            spread(t, j)
     for t in range(2):
         arrive(t, 1)
     for t in range(2):
@@ -279,48 +320,60 @@
     rs(0, 2); rs(1, 1)
     for t in range(2):
         partial(t, 2)
+    rs(0, 3); rs(1, 2); rs(2, 0)
+    for t in range(2):
         arrive(t, 3)
-    rs(0, 3); rs(1, 2)
+    settle(0); rs(1, 3); rs(2, 1)
     for t in range(2):
         partial(t, 3)
-    settle(0); rs(1, 3); rs(2, 0)
-    ag(0, 1); settle(1); rs(2, 1); rs(3, 0)
-    ag(0, 2); ag(1, 1); rs(2, 2); rs(3, 1)
-    ag(0, 3); ag(1, 2); rs(2, 3); rs(3, 2)
-    gathered(0); ag(1, 3); settle(2); rs(3, 3)
+    ag(0, 1); settle(1); rs(2, 2); rs(3, 0)
+    ag(0, 2); ag(1, 1); rs(2, 3); rs(3, 1)
+    ag(0, 3); ag(1, 2); settle(2); rs(3, 2)
+    gathered(0); ag(1, 3); ag(2, 1); rs(3, 3)
+    gathered(1); ag(2, 2); settle(3)
+    for t in range(2):
+        local[6 + t].wait()
     project(0)
-    gathered(1); ag(2, 1); settle(3)
+    ag(2, 3); ag(3, 1)
+    project(1)
     weight_grads(0)
-    ag(2, 2); ag(3, 1)
-    project(1)
+    gathered(2); ag(3, 2)
     weight_grads(1)
-    ag(2, 3); ag(3, 2)
-    gathered(2); ag(3, 3)
+    ag(3, 3)
     project(2)
     weight_grads(2)
     gathered(3)
     project(3)
     weight_grads(3)
-
-    for t in range(2):
-        def add(p, carry, t=t):
-            out = remote(osnd.at[t, p], orcv.at[t, p], out_s.at[t, p], out_r.at[t, p], sib)
-            out.wait_recv()
-            osum[t] = osum[t] + dec(orcv[t, p])
-            return carry
-
-        lax.fori_loop(1, 16, add, 0)
+    for t in range(2):
+        for ab in range(2):
+            rows = pl.ds(ab * SUB, SUB)
+
+            def add(n, carry, t=t, ab=ab, rows=rows):
+                remote(
+                    osnd.at[t, ab, n], orcv.at[t, ab, n], out_s.at[t, ab, n], out_r.at[t, ab, n], sib
+                ).wait_recv()
+                osum[t, rows, :] = osum[t, rows, :] + dec(orcv[t, ab, n])
+                return carry
+
+            lax.fori_loop(1, 16, add, 0)
     out_ref[...] = osum[0] * (1.0 / OUT_SCALE)
     gt_ref[...] = osum[1] * (1.0 / OUT_SCALE)
 
     for t in range(2):
         w_copies[t].wait_send()
-        for p in range(1, 16):
-            tok_copy(t, p).wait_send()
-            out_copy(t, p).wait_send()
+        for ab in range(2):
+            for i in range(1, 4):
+                one_copy(t, ab, i).wait_send()
+                two_copy(t, ab, i).wait_send()
+            for n in range(1, 16):
+                out_copy(t, ab, n).wait_send()
+        for i in range(8):
+            last_copy(t, i, last_block(i)).wait_send()
         for k in range(NCH):
             fwd_copy(t, k).wait_send()
-            sib_copy(t, k).wait_send()
+            if k < NCH - 1:
+                sib_copy(t, k).wait_send()
             for d in range(2):
                 for r in range(4):
                     rs_copy(t, k, d, r).wait_send()
@@ -333,14 +386,16 @@
     return pl.pallas_call(
         kernel,
         out_shape=(
-            jax.ShapeDtypeStruct((BLK, WID), F32),
-            jax.ShapeDtypeStruct((BLK, WID), F32),
-            jax.ShapeDtypeStruct((WID, HID), F32),
-            jax.ShapeDtypeStruct((HID, WID), F32),
+            pltpu.VMEM((BLK, WID), F32),
+            pltpu.VMEM((BLK, WID), F32),
+            pltpu.VMEM((WID, HID), F32),
+            pltpu.VMEM((HID, WID), F32),
         ),
-        in_specs=[vmem] * 4,
+        in_specs=[pl.BlockSpec(memory_space=pl.ANY)] * 4,
         out_specs=(vmem,) * 4,
         scratch_shapes=[
+            pltpu.VMEM((WID, HID), BF16),
+            pltpu.VMEM((HID, WID), BF16),
             pltpu.VMEM((2, NCH * CHR, HID), BF16),
             pltpu.VMEM((2, NCH * CHR, HALF), BF16),
             pltpu.VMEM((HALF, HALF), BF16),
@@ -349,17 +404,19 @@
             pltpu.VMEM((2, NCH, 2, 4, RZ, HALF), BF16),
             pltpu.VMEM((2, NCH, 2, 4, RZ, HALF), BF16),
             pltpu.VMEM((RZ, HALF), F32),
-            pltpu.VMEM((2, 16, BLK, WID), BF16),
-            pltpu.VMEM((2, 16, BLK, WID), BF16),
+            pltpu.VMEM((2, 2, 16, SUB, WID), BF16),
+            pltpu.VMEM((2, 2, 16, SUB, WID), BF16),
             pltpu.VMEM((2, BLK, WID), F32),
-            dma((4,)),
-            dma((2, 16)), dma((2, 16)),
+            dma((8,)),
+            dma((2, 2, 4)), dma((2, 2, 4)),
+            dma((2, 2, 4)), dma((2, 2, 4)),
             dma((2, NCH)), dma((2, NCH)),
             dma((2,)), dma((2,)),
             dma((2, NCH, 2, 4)), dma((2, NCH, 2, 4)),
             dma((2, NCH, 2, 4)), dma((2, NCH, 2, 4)),
             dma((2, NCH)), dma((2, NCH)),
-            dma((2, 16)), dma((2, 16)),
+            dma((2, 8)), dma((2, 8)),
+            dma((2, 2, 16)), dma((2, 2, 16)),
         ],
         compiler_params=pltpu.CompilerParams(
             collective_id=0, has_side_effects=True, vmem_limit_bytes=56 * 2**20

time: 129 us -> 114 us (0.88); the launches traced: 129 us -> 111 us
  Pallas kernels: 121 us -> 107 us
  local copies, waits for them, and re-layouts: 7.86 us -> 4.09 us
    pallas_call x1, Pallas kernels: 121 us -> 107 us  [shards(): pl.pallas_call(kernel, out_shape=(pltpu.VMEM((BLK, WID), F32), pltpu.VMEM...]
    unnamed x6 -> x4, local copies, waits for them, and re-layouts: 7.86 us -> 4.09 us
where the time goes in v2:
time: 114 us; the launch traced here: 111 us
  Pallas kernels  107 us (94%)
  local copies, waits for them, and re-layouts  4.09 us (4%)
    pallas_call x1, Pallas kernels, shards(): pl.pallas_call(kernel, out_shape=(pltpu.VMEM((BLK, WID), F32), pltpu.VMEM...  107 us
    unnamed x4, local copies, waits for them, and re-layouts  4.09 us

profile of v2, /device:TPU:1, one launch (start us, length us, event | category | flops | bytes accessed | tf_op | source)
XLA Modules:
  0.0 111.3 jit_solution(3173639968068740030)
XLA Ops:
  0.6 106.6 %shard_map.75 = (f32[64,384]{1,0:T(8,128)S(1)}, f32[64,384]{1,0:T(8,128)S(1)}, f32[384,1536]{1,0:T(8,128)S(1)}, f32[1536,384]{1,0:T(8,128)S(1)}) custom-call(bf16[64,384]{1,0:T(8,128)(2,1)} %tok_ref.1, bf16[384,1536]{1,0:T(8,128)(2,1)} %win_hbm.1, bf16[1536,384]{1,0:T(8,128)(2,1)} %wout_hbm.1, bf16[64,384]{1,0:T(8,128)(2,1)} %dout_ref.1), custom_call_target="tpu_custom_call" | custom-call | tf_op jit(solution)/shard_map/pallas_call | solution.py:386
  107.2 0.6 copy.12
  107.9 0.6 copy.13
  108.5 1.4 %copy.14 = f32[384,1536]{1,0:T(8,128)} copy(f32[384,1536]{1,0:T(8,128)S(1)} %get-tuple-element.6) | data formatting | bytes 4718592
  109.9 1.4 %copy.15 = f32[1536,384]{1,0:T(8,128)} copy(f32[1536,384]{1,0:T(8,128)S(1)} %get-tuple-element.7) | data formatting | bytes 4718592

commit v3 on v2

--- a/solution.py
+++ b/solution.py
@@ -23,6 +23,7 @@
 STEPS = [0, 1, 3, 2]
 PART = CHR // 2
 SUB = BLK // 2
+BLOCKWISE = (1, 2, 3)
 
 
 def gelu_exact(values):
@@ -49,7 +50,7 @@
     out_ref, gt_ref, gwi_ref, gwo_ref,
     win_ref, wout_ref, acts, xs, wc0, wc1, part, snd, rcv, hid, osnd, orcv, osum,
     loc_sem, one_s, one_r, two_s, two_r, fwd_s, fwd_r, w_s, w_r,
-    rs_s, rs_r, ag_s, ag_r, sib_s, sib_r, last_s, last_r, out_s, out_r,
+    rs_s, rs_r, ag_s, ag_r, sib_s, sib_r, blk_s, blk_r, out_s, out_r,
 ):
     row = lax.axis_index("row")
     col = lax.axis_index("col")
@@ -140,18 +141,11 @@
         fwd_copy(t, k).wait_recv()
         rows = pl.ds(k * CHR, CHR)
 
-        def tile(n, carry):
-            cols = pl.ds(pl.multiple_of(n * 256, 256), 256)
-            if t == 0:
-                got = jnp.dot(xs[0, rows, :], wc0[:, cols], preferred_element_type=F32)
-            else:
-                got = lax.dot_general(
-                    xs[1, rows, :], wc1[cols, :], (((1,), (1,)), ((), ())), preferred_element_type=F32
-                )
-            part[t, k, :, cols] = got * SUM_SCALE
-            return carry
-
-        lax.fori_loop(0, HALF // 256, tile, 0)
+        if t == 0:
+            got = jnp.dot(xs[0, rows, :], wc0[...], preferred_element_type=F32)
+        else:
+            got = lax.dot_general(xs[1, rows, :], wc1[...], (((1,), (1,)), ((), ())), preferred_element_type=F32)
+        part[t, k] = got * SUM_SCALE
 
     def rs_copy(t, k, d, r):
         at = (t, k, d, r)
@@ -206,8 +200,8 @@
                 ag_wait(t, k, d, r - 1)
             block = shift(-r if d == 0 else r)
             ag_copy(t, k, d, r, block).start()
-            if k == NCH - 1 and (r or d == 0):
-                last_copy(t, d * 3 + r, block).start()
+            if k in BLOCKWISE and (r or d == 0):
+                blk_copy(t, k, d * 3 + r, block).start()
 
     def ag(k, r):
         both(lambda t: ag_one(t, k, r))
@@ -230,20 +224,21 @@
         place = acts.at[t, pl.ds(k * CHR, CHR), own_h]
         return remote(place, place, sib_s.at[t, k], sib_r.at[t, k], sib)
 
-    def last_copy(t, i, block):
-        rows = pl.ds(pl.multiple_of((NCH - 1) * CHR + block * RZ, RZ), RZ)
+    def blk_copy(t, k, i, block):
+        rows = pl.ds(pl.multiple_of(k * CHR + block * RZ, RZ), RZ)
         place = acts.at[t, rows, own_h]
-        return remote(place, place, last_s.at[t, i], last_r.at[t, i], sib)
-
-    def last_block(i):
+        at = (t, k - BLOCKWISE[0], i)
+        return remote(place, place, blk_s.at[at], blk_r.at[at], sib)
+
+    def block_at(i):
         return shift(-i if i < 4 else i - 3) if i < 7 else shift(4)
 
     def gathered(k):
         for t in range(2):
             for d in range(2):
                 ag_wait(t, k, d, 3)
-            if k == NCH - 1:
-                last_copy(t, 7, shift(4)).start()
+            if k in BLOCKWISE:
+                blk_copy(t, k, 7, shift(4)).start()
             else:
                 sib_copy(t, k).start()
 
@@ -255,9 +250,9 @@
     def project(k):
         rows = pl.ds(k * CHR, CHR)
         for t in range(2):
-            if k == NCH - 1:
+            if k in BLOCKWISE:
                 for i in range(8):
-                    last_copy(t, i, last_block(i)).wait_recv()
+                    blk_copy(t, k, i, block_at(i)).wait_recv()
             else:
                 sib_copy(t, k).wait_recv()
             if t == 0:
@@ -277,8 +272,8 @@
                         osnd[t, ab, n] = enc(block)
                         out_copy(t, ab, n).start()
 
-    def weight_grads(k):
-        rows = pl.ds(k * CHR, CHR)
+    def grad_w_out(k):
+        rows = pl.ds(k * CHR, 2 * CHR)
 
         def tile(n, carry):
             cols = pl.ds(pl.multiple_of(n * 256, 256), 256)
@@ -286,6 +281,15 @@
                 acts[0, rows, cols], xs[1, rows, own_w], (((0,), (0,)), ((), ())), preferred_element_type=F32
             )
             gwo_ref[cols, :] = more if k == 0 else gwo_ref[cols, :] + more
+            return carry
+
+        lax.fori_loop(0, HID // 256, tile, 0)
+
+    def grad_w_in(k):
+        rows = pl.ds(k * CHR, 2 * CHR)
+
+        def tile(n, carry):
+            cols = pl.ds(pl.multiple_of(n * 256, 256), 256)
             more = lax.dot_general(
                 xs[0, rows, own_w], acts[1, rows, cols], (((0,), (0,)), ((), ())), preferred_element_type=F32
             )
@@ -302,49 +306,50 @@
     for t in range(2):
         arrive(t, 0)
         spread(t, 1)
+        spread(t, 2)
     for t in range(2):
         local[4 + t].wait()
         w_copies[t].wait_recv()
         partial(t, 0)
         rs_one(t, 0, 0)
-    for j in range(2, NCH):
-        for t in range(2):
-            spread(t, j)
     for t in range(2):
         arrive(t, 1)
+        arrive(t, 2)
+        spread(t, 3)
+    rs(0, 1)
     for t in range(2):
         partial(t, 1)
-    rs(0, 1); rs(1, 0)
-    for t in range(2):
-        arrive(t, 2)
-    rs(0, 2); rs(1, 1)
+        rs_one(t, 1, 0)
+    rs(0, 2)
     for t in range(2):
         partial(t, 2)
-    rs(0, 3); rs(1, 2); rs(2, 0)
+        rs_one(t, 2, 0)
+    rs(1, 1)
+    rs(0, 3); rs(1, 2); rs(2, 1)
     for t in range(2):
         arrive(t, 3)
-    settle(0); rs(1, 3); rs(2, 1)
+    settle(0); rs(1, 3); rs(2, 2)
     for t in range(2):
         partial(t, 3)
-    ag(0, 1); settle(1); rs(2, 2); rs(3, 0)
-    ag(0, 2); ag(1, 1); rs(2, 3); rs(3, 1)
-    ag(0, 3); ag(1, 2); settle(2); rs(3, 2)
-    gathered(0); ag(1, 3); ag(2, 1); rs(3, 3)
-    gathered(1); ag(2, 2); settle(3)
+        rs_one(t, 3, 0)
+    ag(0, 1); settle(1); rs(2, 3); rs(3, 1)
+    ag(0, 2); ag(1, 1); settle(2); rs(3, 2)
+    ag(0, 3); ag(1, 2); ag(2, 1); rs(3, 3)
     for t in range(2):
         local[6 + t].wait()
+    gathered(0); ag(1, 3); ag(2, 2); settle(3)
     project(0)
-    ag(2, 3); ag(3, 1)
+    gathered(1); ag(2, 3); ag(3, 1)
     project(1)
-    weight_grads(0)
     gathered(2); ag(3, 2)
-    weight_grads(1)
+    project(2)
     ag(3, 3)
-    project(2)
-    weight_grads(2)
+    grad_w_out(0)
     gathered(3)
     project(3)
-    weight_grads(3)
+    grad_w_in(0)
+    grad_w_out(2)
+    grad_w_in(2)
     for t in range(2):
         for ab in range(2):
             rows = pl.ds(ab * SUB, SUB)
@@ -368,11 +373,12 @@
                 two_copy(t, ab, i).wait_send()
             for n in range(1, 16):
                 out_copy(t, ab, n).wait_send()
-        for i in range(8):
-            last_copy(t, i, last_block(i)).wait_send()
         for k in range(NCH):
             fwd_copy(t, k).wait_send()
-            if k < NCH - 1:
+            if k in BLOCKWISE:
+                for i in range(8):
+                    blk_copy(t, k, i, block_at(i)).wait_send()
+            else:
                 sib_copy(t, k).wait_send()
             for d in range(2):
                 for r in range(4):
@@ -380,17 +386,22 @@
                     ag_copy(t, k, d, r, shift(-r if d == 0 else r)).wait_send()
 
 
+def store(out_v, gt_v, gwi_v, gwo_v, out_ref, gt_ref, gwi_ref, gwo_ref, sems):
+    pairs = [(gwi_v, gwi_ref), (gwo_v, gwo_ref), (out_v, out_ref), (gt_v, gt_ref)]
+    copies = [pltpu.make_async_copy(a, b, sems.at[i]) for i, (a, b) in enumerate(pairs)]
+    for c in copies:
+        c.start()
+    for c in copies:
+        c.wait()
+
+
 def shards(tokens, w_in, w_out, d_output):
     vmem = pl.BlockSpec(memory_space=pltpu.VMEM)
     dma = pltpu.SemaphoreType.DMA
-    return pl.pallas_call(
+    shapes = [(BLK, WID), (BLK, WID), (WID, HID), (HID, WID)]
+    results = pl.pallas_call(
         kernel,
-        out_shape=(
-            pltpu.VMEM((BLK, WID), F32),
-            pltpu.VMEM((BLK, WID), F32),
-            pltpu.VMEM((WID, HID), F32),
-            pltpu.VMEM((HID, WID), F32),
-        ),
+        out_shape=tuple(pltpu.VMEM(shape, F32) for shape in shapes),
         in_specs=[pl.BlockSpec(memory_space=pl.ANY)] * 4,
         out_specs=(vmem,) * 4,
         scratch_shapes=[
@@ -415,13 +426,21 @@
             dma((2, NCH, 2, 4)), dma((2, NCH, 2, 4)),
             dma((2, NCH, 2, 4)), dma((2, NCH, 2, 4)),
             dma((2, NCH)), dma((2, NCH)),
-            dma((2, 8)), dma((2, 8)),
+            dma((2, 3, 8)), dma((2, 3, 8)),
             dma((2, 2, 16)), dma((2, 2, 16)),
         ],
         compiler_params=pltpu.CompilerParams(
             collective_id=0, has_side_effects=True, vmem_limit_bytes=56 * 2**20
         ),
     )(tokens, w_in, w_out, d_output)
+    return pl.pallas_call(
+        store,
+        out_shape=tuple(jax.ShapeDtypeStruct(shape, F32) for shape in shapes),
+        in_specs=[pl.BlockSpec(memory_space=pl.ANY)] * 4,
+        out_specs=(pl.BlockSpec(memory_space=pl.ANY),) * 4,
+        scratch_shapes=[dma((4,))],
+        compiler_params=pltpu.CompilerParams(vmem_limit_bytes=2**20),
+    )(*results)
 
 
 def solution(mesh):

time: 114 us -> 106 us (0.930); the launches traced: 111 us -> 106 us
  local copies, waits for them, and re-layouts: 4.09 us -> 0 us
  Pallas kernels: 107 us -> 105 us
    unnamed x4 -> x0, local copies, waits for them, and re-layouts: 4.09 us -> none
    pallas_call x1 -> x2, Pallas kernels: 107 us -> 105 us  [the longest x1 103 us: shards(): pl.pallas_call(kernel, out_shape=tuple((pltpu.VMEM(shape, F32) for shape...]
where the time goes in v3:
time: 106 us
  Pallas kernels  105 us (99%)
    pallas_call x1, Pallas kernels, shards(): pl.pallas_call(kernel, out_shape=tuple((pltpu.VMEM(shape, F32) for shape...  103 us
    pallas_call x1, Pallas kernels, shards(): pl.pallas_call(store, out_shape=tuple((jax.ShapeDtypeStruct(shape, F32) f...  2.26 us

profile of v3, /device:TPU:1, one launch (start us, length us, event | category | flops | bytes accessed | tf_op | source)
XLA Modules:
  0.0 105.5 jit_solution(14074110593832364006)
XLA Ops:
  0.6 102.6 %shard_map.75 = (f32[64,384]{1,0:T(8,128)S(1)}, f32[64,384]{1,0:T(8,128)S(1)}, f32[384,1536]{1,0:T(8,128)S(1)}, f32[1536,384]{1,0:T(8,128)S(1)}) custom-call(bf16[64,384]{1,0:T(8,128)(2,1)} %tok_ref.1, bf16[384,1536]{1,0:T(8,128)(2,1)} %win_hbm.1, bf16[1536,384]{1,0:T(8,128)(2,1)} %wout_hbm.1, bf16[64,384]{1,0:T(8,128)(2,1)} %dout_ref.1), custom_call_target="tpu_custom_call" | custom-call | tf_op jit(solution)/shard_map/pallas_call | solution.py:402
  103.3 2.3 %shard_map.76 = (f32[64,384]{1,0:T(8,128)}, f32[64,384]{1,0:T(8,128)}, f32[384,1536]{1,0:T(8,128)}, f32[1536,384]{1,0:T(8,128)}) custom-call(f32[64,384]{1,0:T(8,128)S(1)} %get-tuple-element.8.out_v, f32[64,384]{1,0:T(8,128)S(1)} %get-tuple-element.9.gt_v, f32[384,1536]{1,0:T(8,128)S(1)} %get-tuple-element.10.gwi_v, f32[1536,384]{1,0:T(8,128)S(1)} %get-tuple-element.11.gwo_v), custom_call_target="tpu_custom_call" | custom-call | tf_op jit(solution)/shard_map/pallas_call | solution.py:436

commit v4 on v3

--- a/solution.py
+++ b/solution.py
@@ -23,7 +23,7 @@
 STEPS = [0, 1, 3, 2]
 PART = CHR // 2
 SUB = BLK // 2
-BLOCKWISE = (1, 2, 3)
+BLOCKWISE = (2, 3)
 
 
 def gelu_exact(values):
@@ -247,9 +247,9 @@
         to = peer(near, far) if ab == 0 else peer(far, near)
         return remote(osnd.at[t, ab, n], orcv.at[t, ab, n], out_s.at[t, ab, n], out_r.at[t, ab, n], to)
 
-    def project(k):
+    def project(k, ts=(0, 1)):
         rows = pl.ds(k * CHR, CHR)
-        for t in range(2):
+        for t in ts:
             if k in BLOCKWISE:
                 for i in range(8):
                     blk_copy(t, k, i, block_at(i)).wait_recv()
@@ -314,12 +314,13 @@
         rs_one(t, 0, 0)
     for t in range(2):
         arrive(t, 1)
+        rs_one(t, 0, 1)
+    for t in range(2):
+        partial(t, 1)
+        rs_one(t, 1, 0)
+    for t in range(2):
         arrive(t, 2)
         spread(t, 3)
-    rs(0, 1)
-    for t in range(2):
-        partial(t, 1)
-        rs_one(t, 1, 0)
     rs(0, 2)
     for t in range(2):
         partial(t, 2)
@@ -340,13 +341,15 @@
     gathered(0); ag(1, 3); ag(2, 2); settle(3)
     project(0)
     gathered(1); ag(2, 3); ag(3, 1)
-    project(1)
+    project(1, (0,))
     gathered(2); ag(3, 2)
-    project(2)
+    project(1, (1,))
+    project(2, (0,))
     ag(3, 3)
-    grad_w_out(0)
+    project(2, (1,))
     gathered(3)
     project(3)
+    grad_w_out(0)
     grad_w_in(0)
     grad_w_out(2)
     grad_w_in(2)
@@ -426,7 +429,7 @@
             dma((2, NCH, 2, 4)), dma((2, NCH, 2, 4)),
             dma((2, NCH, 2, 4)), dma((2, NCH, 2, 4)),
             dma((2, NCH)), dma((2, NCH)),
-            dma((2, 3, 8)), dma((2, 3, 8)),
+            dma((2, 2, 8)), dma((2, 2, 8)),
             dma((2, 2, 16)), dma((2, 2, 16)),
         ],
         compiler_params=pltpu.CompilerParams(

time: 106 us -> 105 us (level)
    pallas_call x1, Pallas kernels: 103 us -> 101 us  [shards(): pl.pallas_call(kernel, out_shape=tuple((pltpu.VMEM(shape, F32) for shape...]
where the time goes in v4:
time: 105 us; the launch traced here: 104 us
  Pallas kernels  104 us (99%)
    pallas_call x1, Pallas kernels, shards(): pl.pallas_call(kernel, out_shape=tuple((pltpu.VMEM(shape, F32) for shape...  101 us
    pallas_call x1, Pallas kernels, shards(): pl.pallas_call(store, out_shape=tuple((jax.ShapeDtypeStruct(shape, F32) f...  2.26 us

profile of v4, /device:TPU:1, one launch (start us, length us, event | category | flops | bytes accessed | tf_op | source)
XLA Modules:
  0.0 104.4 jit_solution(1878046655838121599)
XLA Ops:
  0.6 101.4 %shard_map.75 = (f32[64,384]{1,0:T(8,128)S(1)}, f32[64,384]{1,0:T(8,128)S(1)}, f32[384,1536]{1,0:T(8,128)S(1)}, f32[1536,384]{1,0:T(8,128)S(1)}) custom-call(bf16[64,384]{1,0:T(8,128)(2,1)} %tok_ref.1, bf16[384,1536]{1,0:T(8,128)(2,1)} %win_hbm.1, bf16[1536,384]{1,0:T(8,128)(2,1)} %wout_hbm.1, bf16[64,384]{1,0:T(8,128)(2,1)} %dout_ref.1), custom_call_target="tpu_custom_call" | custom-call | tf_op jit(solution)/shard_map/pallas_call | solution.py:405
  102.0 2.3 %shard_map.76 = (f32[64,384]{1,0:T(8,128)}, f32[64,384]{1,0:T(8,128)}, f32[384,1536]{1,0:T(8,128)}, f32[1536,384]{1,0:T(8,128)}) custom-call(f32[64,384]{1,0:T(8,128)S(1)} %get-tuple-element.8.out_v, f32[64,384]{1,0:T(8,128)S(1)} %get-tuple-element.9.gt_v, f32[384,1536]{1,0:T(8,128)S(1)} %get-tuple-element.10.gwi_v, f32[1536,384]{1,0:T(8,128)S(1)} %get-tuple-element.11.gwo_v), custom_call_target="tpu_custom_call" | custom-call | tf_op jit(solution)/shard_map/pallas_call | solution.py:439

commit v5 on v4

--- a/solution.py
+++ b/solution.py
@@ -114,9 +114,9 @@
             two_s.at[t, ab, j], two_r.at[t, ab, j], to,
         )
 
-    def fwd_copy(t, k):
-        place = xs.at[t, pl.ds(k * CHR, CHR), own_w]
-        return remote(place, place, fwd_s.at[t, k], fwd_r.at[t, k], sib)
+    def fwd_copy(t, k, ab):
+        place = xs.at[t, pl.ds(k * CHR + ab * PART, PART), own_w]
+        return remote(place, place, fwd_s.at[t, k, ab], fwd_r.at[t, k, ab], sib)
 
     w_copies = [
         remote(win_hbm.at[:, oth_h], wc0.at[own_w, :], w_s.at[0], w_r.at[0], sib),
@@ -135,10 +135,11 @@
                 local[t * 2 + ab].wait()
                 for i in range(1, 4):
                     one_copy(t, ab, i).wait_recv()
-        fwd_copy(t, k).start()
+            fwd_copy(t, k, ab).start()
 
     def partial(t, k):
-        fwd_copy(t, k).wait_recv()
+        for ab in range(2):
+            fwd_copy(t, k, ab).wait_recv()
         rows = pl.ds(k * CHR, CHR)
 
         if t == 0:
@@ -249,18 +250,22 @@
 
     def project(k, ts=(0, 1)):
         rows = pl.ds(k * CHR, CHR)
-        for t in ts:
+
+        def product(t, cols):
+            if t == 0:
+                return jnp.dot(acts[0, rows, cols], wout_ref[cols, :], preferred_element_type=F32)
+            return lax.dot_general(
+                acts[1, rows, cols], win_ref[:, cols], (((1,), (1,)), ((), ())), preferred_element_type=F32
+            )
+
+        first = [product(t, own_h) for t in ts]
+        for t, got in zip(ts, first):
             if k in BLOCKWISE:
                 for i in range(8):
                     blk_copy(t, k, i, block_at(i)).wait_recv()
             else:
                 sib_copy(t, k).wait_recv()
-            if t == 0:
-                got = jnp.dot(acts[0, rows, :], wout_ref[...], preferred_element_type=F32)
-            else:
-                got = lax.dot_general(
-                    acts[1, rows, :], win_ref[...], (((1,), (1,)), ((), ())), preferred_element_type=F32
-                )
+            got = got + product(t, oth_h)
             got = got * OUT_SCALE
             for ab in range(2):
                 for i in range(4):
@@ -377,7 +382,8 @@
             for n in range(1, 16):
                 out_copy(t, ab, n).wait_send()
         for k in range(NCH):
-            fwd_copy(t, k).wait_send()
+            for ab in range(2):
+                fwd_copy(t, k, ab).wait_send()
             if k in BLOCKWISE:
                 for i in range(8):
                     blk_copy(t, k, i, block_at(i)).wait_send()
@@ -424,7 +430,7 @@
             dma((8,)),
             dma((2, 2, 4)), dma((2, 2, 4)),
             dma((2, 2, 4)), dma((2, 2, 4)),
-            dma((2, NCH)), dma((2, NCH)),
+            dma((2, NCH, 2)), dma((2, NCH, 2)),
             dma((2,)), dma((2,)),
             dma((2, NCH, 2, 4)), dma((2, NCH, 2, 4)),
             dma((2, NCH, 2, 4)), dma((2, NCH, 2, 4)),

time: 105 us -> 105 us (level)
  no operation moved by 1% of the time
where the time goes in v5:
time: 105 us
  Pallas kernels  104 us (99%)
    pallas_call x1, Pallas kernels, shards(): pl.pallas_call(kernel, out_shape=tuple((pltpu.VMEM(shape, F32) for shape...  102 us
    pallas_call x1, Pallas kernels, shards(): pl.pallas_call(store, out_shape=tuple((jax.ShapeDtypeStruct(shape, F32) f...  2.26 us

profile of v5, /device:TPU:1, one launch (start us, length us, event | category | flops | bytes accessed | tf_op | source)
XLA Modules:
  0.0 104.6 jit_solution(14533899434915744197)
XLA Ops:
  0.6 101.6 %shard_map.75 = (f32[64,384]{1,0:T(8,128)S(1)}, f32[64,384]{1,0:T(8,128)S(1)}, f32[384,1536]{1,0:T(8,128)S(1)}, f32[1536,384]{1,0:T(8,128)S(1)}) custom-call(bf16[64,384]{1,0:T(8,128)(2,1)} %tok_ref.1, bf16[384,1536]{1,0:T(8,128)(2,1)} %win_hbm.1, bf16[1536,384]{1,0:T(8,128)(2,1)} %wout_hbm.1, bf16[64,384]{1,0:T(8,128)(2,1)} %dout_ref.1), custom_call_target="tpu_custom_call" | custom-call | tf_op jit(solution)/shard_map/pallas_call | solution.py:411
  102.2 2.3 %shard_map.76 = (f32[64,384]{1,0:T(8,128)}, f32[64,384]{1,0:T(8,128)}, f32[384,1536]{1,0:T(8,128)}, f32[1536,384]{1,0:T(8,128)}) custom-call(f32[64,384]{1,0:T(8,128)S(1)} %get-tuple-element.8.out_v, f32[64,384]{1,0:T(8,128)S(1)} %get-tuple-element.9.gt_v, f32[384,1536]{1,0:T(8,128)S(1)} %get-tuple-element.10.gwi_v, f32[1536,384]{1,0:T(8,128)S(1)} %get-tuple-element.11.gwo_v), custom_call_target="tpu_custom_call" | custom-call | tf_op jit(solution)/shard_map/pallas_call | solution.py:445
